TPU v7x, 32 devices: a whole 2x2x4 slice. The times are simulated.
32 devices in a mesh: seq: 16 (over z, y, core), pair: 2 (over x).
Axes of the slice: x: 2, y: 2, z: 4, core: 2. Of those that a mesh axis runs over, the one named last changes fastest.
Arguments:
- student: float32 [10240, 1408], P('seq'), may hold values from -640 to 640
- teacher: float32 [10240, 1408], P('seq'), may hold values from -640 to 640
Outputs:
- student_grad: float32 [10240, 1408], P('seq')
All inputs are finite; a program needn't handle non-finite values.
Results may differ from a plain program's by a relative error of at most 0.0059.
Values may be sent and summed in bfloat16 or wider, within the bound.
No kernel may reach another device: no remote copies, remote signals or barrier semaphores. Data moves between devices by JAX's collectives and lax.ppermute only.
A program may use at most 64 MiB of HBM per device.

v0:
```python
import functools
import math

import jax
import jax.numpy as jnp
from jax import lax
from jax.experimental import pallas as pl
from jax.experimental.pallas import tpu as pltpu
from jax.sharding import PartitionSpec as P

CORES = 2
ROW_TILE = 16
VMEM_LIMIT = 48 * 1024 * 1024


def normalize(values, width):
    scale = lax.rsqrt(jnp.sum(values * values, axis=1, keepdims=True) + width * 1e-06)
    return (scale, values * scale)


def relation_kernel(margin, weight, counts, has_total, last, *refs):
    refs = list(refs)
    own_s, own_t = refs[:2]
    partners = refs[2 : 2 + 2 * len(counts)]
    rest = refs[2 + 2 * len(counts) :]
    total = rest.pop(0) if has_total else None
    student, scale = (rest.pop(0), rest.pop(0)) if last else (None, None)
    out, all_s, all_t = rest

    @pl.when(pl.program_id(0) == 0)
    def _():
        at = 0
        for k, count in enumerate(counts):
            all_s[at : at + count, :] = partners[2 * k][...]
            all_t[at : at + count, :] = partners[2 * k + 1][...]
            at += count

    contract = (((1,), (1,)), ((), ()))
    s_rel = lax.dot_general(own_s[...], all_s[...], contract, preferred_element_type=jnp.float32)
    t_rel = lax.dot_general(own_t[...], all_t[...], contract, preferred_element_type=jnp.float32)
    delta = s_rel - t_rel
    shrink = jnp.maximum(delta - margin, 0.0) + jnp.minimum(delta + margin, 0.0)
    relation = (weight * shrink).astype(jnp.bfloat16)
    grad = jnp.dot(relation, all_s[...], preferred_element_type=jnp.float32)
    if has_total:
        grad = total[...] + grad
    if last:
        unit = student[...] * scale[...]
        grad = grad - unit * jnp.sum(unit * grad, axis=1, keepdims=True)
    out[...] = grad.astype(out.dtype)


def add_relation(own, partners, total, final, margin, weight):
    rows, width = own[0].shape
    block = rows // 2
    counts = tuple(s.shape[0] for s, _ in partners)
    tokens = sum(counts)
    flat = [x for pair in partners for x in pair]
    by_row = pl.BlockSpec((block, width), lambda i: (i, 0))
    operands = list(own) + flat
    specs = [by_row, by_row] + [
        pl.BlockSpec(x.shape, lambda i: (0, 0), pipeline_mode=pl.Buffered(1)) for x in flat
    ]
    aliases = {}
    if total is not None:
        if final is None:
            aliases = {len(operands): 0}
        operands.append(total)
        specs.append(by_row)
    if final is not None:
        operands += list(final)
        specs += [by_row, pl.BlockSpec((block, 1), lambda i: (i, 0))]
    dtype = jnp.float32 if final is None else jnp.bfloat16
    return pl.pallas_call(
        functools.partial(
            relation_kernel, margin, weight, counts, total is not None, final is not None
        ),
        grid=(rows // block,),
        in_specs=specs,
        out_specs=by_row,
        out_shape=jax.ShapeDtypeStruct((rows, width), dtype),
        scratch_shapes=[pltpu.VMEM((tokens, width), jnp.bfloat16)] * 2,
        input_output_aliases=aliases,
        compiler_params=pltpu.CompilerParams(vmem_limit_bytes=VMEM_LIMIT),
        cost_estimate=pl.CostEstimate(
            flops=6 * rows * tokens * width,
            bytes_accessed=4 * rows * width + 4 * tokens * width + 8 * rows * width,
            transcendentals=0,
        ),
    )(*operands)


def sum_over_pair(half, count):
    distance = 1
    value = half
    while distance < count:
        half = value.astype(jnp.bfloat16)
        other = lax.ppermute(half, "pair", [(i, i ^ distance) for i in range(count)])
        value = half.astype(jnp.float32) + other.astype(jnp.float32)
        distance *= 2
    return value


def ring_routes(count):
    chips = count // CORES
    order = list(range(0, chips, 2)) + list(range(1, chips, 2))[::-1]
    onward, back = [], []
    for place, chip in enumerate(order):
        following = order[(place + 1) % chips]
        for core in range(CORES):
            onward.append((chip * CORES + core, following * CORES + core))
            back.append((following * CORES + core, chip * CORES + core))
    swap = [(i, i ^ 1) for i in range(count)]
    return onward, back, swap


def local(student, teacher):
    rows, width = student.shape
    seq_count = lax.axis_size("seq")
    pair_count = lax.axis_size("pair")
    pair_index = lax.axis_index("pair")
    margin = 0.75 / math.sqrt(width)
    weight = 64.0 * width / math.sqrt(rows * seq_count)
    s_scale, s_unit = normalize(student, width)
    t_scale, t_unit = normalize(teacher, width)
    s_half = s_unit.astype(jnp.bfloat16)
    t_half = t_unit.astype(jnp.bfloat16)
    share = rows // pair_count
    first = -(-share // (2 * ROW_TILE)) * ROW_TILE
    onward, back, swap = ring_routes(seq_count)

    def send(parts, route):
        return tuple(lax.ppermute(part, "seq", route) for part in parts)

    def add(partners, total, final=None):
        return add_relation((s_half, t_half), partners, total, final, margin, weight)

    start = pair_index * share
    own = tuple(lax.dynamic_slice_in_dim(x, start, share, 0) for x in (s_half, t_half))
    total = add([own, send(own, swap)], None)
    onto, off = own, own
    hops = seq_count // CORES // 2
    for hop in range(1, hops + 1):
        final = None
        if hop == hops:
            onto = tuple(x[:first] for x in onto)
            off = tuple(x[first:] for x in off)
            final = (student, s_scale)
        onto, off = send(onto, onward), send(off, back)
        total = add([onto, off, send(onto, swap), send(off, swap)], total, final)
    return s_scale * sum_over_pair(total, pair_count)


def solution(mesh):
    placed = (P("seq", None), P("seq", None))
    return jax.shard_map(
        local, mesh=mesh, in_specs=placed, out_specs=P("seq", None), check_vma=False
    )
```

profile of v0, /device:TPU:0, one launch (start us, length us, event | category | flops | bytes accessed | tf_op | source)
XLA Modules:
  0.0 240.2 jit_solution(17165669015967502557)
XLA Ops:
  0.0 2.5 %multiply_reduce_fusion.1 = f32[640]{0:T(1024)S(1)} fusion(f32[640,1408]{1,0:T(8,128)} %refs_11_.1), kind=kLoop, calls=%fused_computation.4 | loop fusion | flops 1801600 | bytes 3607040 | tf_op jit(solution)/shard_map/reduce_sum | solution.py:17
  4.0 2.6 %collective-permute-start = (bf16[320,1408]{1,0:T(8,128)(2,1)S(1)}, bf16[320,1408]{1,0:T(8,128)(2,1)S(1)}, u32[]{:S(2)}, u32[]{:S(2)}) collective-permute-start(bf16[320,1408]{1,0:T(8,128)(2,1)S(1)} %constant_dynamic-slice_fusion.1.refs_2_), channel_id=1, source_target_pairs={{0,8},{2,10},{8,16},{10,18},{16,24},{18,26},{24,28},{26,30},{28,20... | collective-permute-start | bytes 2703368 | tf_op jit(solution)/shard_map/ppermute | solution.py:133
  6.7 2.3 multiply_reduce_fusion
  9.4 2.0 collective-permute-start.4
  12.6 14.9 %collective-permute-done.refs_2_ = bf16[320,1408]{1,0:T(8,128)(2,1)S(1)} collective-permute-done((bf16[320,1408]{1,0:T(8,128)(2,1)S(1)}, bf16[320,1408]{1,0:T(8,128)(2,1)S(1)}, u32[]{:S(2)}, u32[]{:S(2)}) %collective-permute-start) | collective-permute-done | bytes 901152 | tf_op jit(solution)/shard_map/ppermute | solution.py:133
  27.4 2.0 collective-permute-done.8.refs_4_
  29.5 17.0 %collective-permute-done.4.refs_3_ = bf16[320,1408]{1,0:T(8,128)(2,1)S(1)} collective-permute-done((bf16[320,1408]{1,0:T(8,128)(2,1)S(1)}, bf16[320,1408]{1,0:T(8,128)(2,1)S(1)}, u32[]{:S(2)}, u32[]{:S(2)}) %collective-permute-start.4) | collective-permute-done | bytes 901152 | tf_op jit(solution)/shard_map/ppermute | solution.py:133
  47.4 1.8 collective-permute-start.1
  50.7 1.8 collective-permute-start.5
  54.7 15.6 %collective-permute-done.1.refs_2_ = bf16[320,1408]{1,0:T(8,128)(2,1)S(1)} collective-permute-done((bf16[320,1408]{1,0:T(8,128)(2,1)S(1)}, bf16[320,1408]{1,0:T(8,128)(2,1)S(1)}, u32[]{:S(2)}, u32[]{:S(2)}) %collective-permute-start.1) | collective-permute-done | bytes 901152 | tf_op jit(solution)/shard_map/ppermute | solution.py:133
  70.3 1.9 collective-permute-start.2
  72.1 1.2 collective-permute-done.9.refs_4_
  73.5 16.1 %collective-permute-done.5.refs_3_ = bf16[320,1408]{1,0:T(8,128)(2,1)} collective-permute-done((bf16[320,1408]{1,0:T(8,128)(2,1)S(1)}, bf16[320,1408]{1,0:T(8,128)(2,1)}, u32[]{:S(2)}, u32[]{:S(2)}) %collective-permute-start.5) | collective-permute-done | bytes 901152 | tf_op jit(solution)/shard_map/ppermute | solution.py:133
  89.7 3.1 %collective-permute-done.13.refs_5_ = bf16[320,1408]{1,0:T(8,128)(2,1)} collective-permute-done((bf16[320,1408]{1,0:T(8,128)(2,1)S(1)}, bf16[320,1408]{1,0:T(8,128)(2,1)}, u32[]{:S(2)}, u32[]{:S(2)}) %collective-permute-start.13) | collective-permute-done | bytes 901152 | tf_op jit(solution)/shard_map/ppermute | solution.py:133
  92.7 1.6 collective-permute-start.6
  95.3 13.6 %collective-permute-done.2.refs_2_ = bf16[320,1408]{1,0:T(8,128)(2,1)S(1)} collective-permute-done((bf16[320,1408]{1,0:T(8,128)(2,1)S(1)}, bf16[320,1408]{1,0:T(8,128)(2,1)S(1)}, u32[]{:S(2)}, u32[]{:S(2)}) %collective-permute-start.2) | collective-permute-done | bytes 901152 | tf_op jit(solution)/shard_map/ppermute | solution.py:133
  108.9 2.4 %collective-permute-done.10.refs_4_ = bf16[320,1408]{1,0:T(8,128)(2,1)S(1)} collective-permute-done((bf16[320,1408]{1,0:T(8,128)(2,1)S(1)}, bf16[320,1408]{1,0:T(8,128)(2,1)S(1)}, u32[]{:S(2)}, u32[]{:S(2)}) %collective-permute-start.10) | collective-permute-done | bytes 901152 | tf_op jit(solution)/shard_map/ppermute | solution.py:133
  111.7 1.8 collective-permute-start.3
  113.5 14.7 %collective-permute-done.6.refs_3_ = bf16[320,1408]{1,0:T(8,128)(2,1)S(1)} collective-permute-done((bf16[320,1408]{1,0:T(8,128)(2,1)}, bf16[320,1408]{1,0:T(8,128)(2,1)S(1)}, u32[]{:S(2)}, u32[]{:S(2)}) %collective-permute-start.6) | collective-permute-done | bytes 901152 | tf_op jit(solution)/shard_map/ppermute | solution.py:133
  128.2 1.7 collective-permute-start.11
  131.3 1.2 copy-done.14
  132.4 7.7 %shard_map.28.refs_10_ = f32[640,1408]{1,0:T(8,128)} custom-call(bf16[640,1408]{1,0:T(8,128)(2,1)S(1)} %multiply_convert_fusion.1.refs_0_, bf16[640,1408]{1,0:T(8,128)(2,1)} %copy-done.19, bf16[320,1408]{1,0:T(8,128)(2,1)S(1)} %constant_dynamic-slice_fusion.1.refs_2_, bf16[320,1408]{1,0:T(8,128)(2,1)S(1)} %constant_dynamic-slice_fusion.refs_3_, ...), custom_call_target="tpu_custom_call" | custom-call | flops 3460300800 | bytes 14417920 | tf_op jit(solution)/shard_map/pallas_call | solution.py:74
  141.1 1.5 collective-permute-done.11.refs_4_
  143.7 1.2 copy-done.10
  144.9 13.1 %shard_map.29.refs_10_ = f32[640,1408]{1,0:T(8,128)} custom-call(bf16[640,1408]{1,0:T(8,128)(2,1)} %copy-done, bf16[640,1408]{1,0:T(8,128)(2,1)} %copy-done.19, bf16[320,1408]{1,0:T(8,128)(2,1)S(1)} %collective-permute-done.refs_2_, bf16[320,1408]{1,0:T(8,128)(2,1)S(1)} %collective-permute-done.4.refs_3_, ...), custom_call_target="tpu_custom_call", output_to_operand_aliasing={{}: (10, {})} | custom-call | flops 6920601600 | bytes 18022400 | tf_op jit(solution)/shard_map/pallas_call | solution.py:74
  159.1 1.2 copy-done.16
  160.2 13.6 %shard_map.30.refs_10_ = f32[640,1408]{1,0:T(8,128)} custom-call(bf16[640,1408]{1,0:T(8,128)(2,1)} %copy-done, bf16[640,1408]{1,0:T(8,128)(2,1)} %copy-done.19, bf16[320,1408]{1,0:T(8,128)(2,1)S(1)} %copy-done.6, bf16[320,1408]{1,0:T(8,128)(2,1)} %collective-permute-done.5.refs_3_, ...), custom_call_target="tpu_custom_call", output_to_operand_aliasing={{}: (10, {})} | custom-call | flops 6920601600 | bytes 18022400 | tf_op jit(solution)/shard_map/pallas_call | solution.py:74
  174.9 13.1 %shard_map.31.refs_10_ = f32[640,1408]{1,0:T(8,128)} custom-call(bf16[640,1408]{1,0:T(8,128)(2,1)} %copy-done, bf16[640,1408]{1,0:T(8,128)(2,1)} %copy-done.19, bf16[320,1408]{1,0:T(8,128)(2,1)S(1)} %collective-permute-done.2.refs_2_, bf16[320,1408]{1,0:T(8,128)(2,1)S(1)} %collective-permute-done.6.refs_3_, ...), custom_call_target="tpu_custom_call", output_to_operand_aliasing={{}: (10, {})} | custom-call | flops 6920601600 | bytes 18022400 | tf_op jit(solution)/shard_map/pallas_call | solution.py:74
  187.9 8.5 %shard_map.32 = bf16[640,1408]{1,0:T(8,128)(2,1)S(1)} custom-call(bf16[640,1408]{1,0:T(8,128)(2,1)} %copy-done, bf16[640,1408]{1,0:T(8,128)(2,1)} %copy-done.19, bf16[160,1408]{1,0:T(8,128)(2,1)S(1)} %collective-permute-done.3.refs_2_, bf16[160,1408]{1,0:T(8,128)(2,1)S(1)} %collective-permute-done.7.refs_3_, ...), custom_call_target="tpu_custom_call" | custom-call | flops 3460300800 | bytes 14417920 | tf_op jit(solution)/shard_map/pallas_call | solution.py:74
  196.4 1.5 collective-permute-start.34
  198.0 39.8 %collective-permute-done.34 = bf16[640,1408]{1,0:T(8,128)(2,1)S(1)} collective-permute-done((bf16[640,1408]{1,0:T(8,128)(2,1)S(1)}, bf16[640,1408]{1,0:T(8,128)(2,1)S(1)}, u32[]{:S(2)}, u32[]{:S(2)}) %collective-permute-start.34) | collective-permute-done | bytes 1802272 | tf_op jit(solution)/shard_map/ppermute | solution.py:98
  237.8 2.4 add_multiply_fusion
  (101 shorter events, 14.6 us)
Async XLA Ops:
  4.0 23.4 %collective-permute-start = (bf16[320,1408]{1,0:T(8,128)(2,1)S(1)}, bf16[320,1408]{1,0:T(8,128)(2,1)S(1)}, u32[]{:S(2)}, u32[]{:S(2)}) collective-permute-start(bf16[320,1408]{1,0:T(8,128)(2,1)S(1)} %constant_dynamic-slice_fusion.1.refs_2_), channel_id=1, source_target_pairs={{0,8},{2,10},{8,16},{10,18},{16,24},{18,26},{24,28},{26,30},{28,20... | collective-permute-start | bytes 2703368 | tf_op jit(solution)/shard_map/ppermute | solution.py:133
  6.6 22.8 %collective-permute-start.8 = (bf16[320,1408]{1,0:T(8,128)(2,1)S(1)}, bf16[320,1408]{1,0:T(8,128)(2,1)S(1)}, u32[]{:S(2)}, u32[]{:S(2)}) collective-permute-start(bf16[320,1408]{1,0:T(8,128)(2,1)S(1)} %constant_dynamic-slice_fusion.1.refs_2_), channel_id=1, source_target_pairs={{8,0},{10,2},{16,8},{18,10},{24,16},{26,18},{28,24},{30,26},{20,28... | collective-permute-start | bytes 2703368 | tf_op jit(solution)/shard_map/ppermute | solution.py:133
  9.4 37.1 %collective-permute-start.4 = (bf16[320,1408]{1,0:T(8,128)(2,1)S(1)}, bf16[320,1408]{1,0:T(8,128)(2,1)S(1)}, u32[]{:S(2)}, u32[]{:S(2)}) collective-permute-start(bf16[320,1408]{1,0:T(8,128)(2,1)S(1)} %constant_dynamic-slice_fusion.refs_3_), channel_id=1, source_target_pairs={{0,8},{2,10},{8,16},{10,18},{16,24},{18,26},{24,28},{26,30},{28,20... | collective-permute-start | bytes 2703368 | tf_op jit(solution)/shard_map/ppermute | solution.py:133
  11.4 35.1 %collective-permute-start.33 = (bf16[320,1408]{1,0:T(8,128)(2,1)S(1)}, bf16[320,1408]{1,0:T(8,128)(2,1)S(1)}, u32[]{:S(2)}, u32[]{:S(2)}) collective-permute-start(bf16[320,1408]{1,0:T(8,128)(2,1)S(1)} %constant_dynamic-slice_fusion.refs_3_), channel_id=1, source_target_pairs={{0,2},{2,0},{4,6},{6,4},{8,10},{10,8},{12,14},{14,12},{16,18},{18,... | collective-permute-start | bytes 2703368 | tf_op jit(solution)/shard_map/ppermute | solution.py:133
  12.4 36.9 %collective-permute-start.12 = (bf16[320,1408]{1,0:T(8,128)(2,1)S(1)}, bf16[320,1408]{1,0:T(8,128)(2,1)S(1)}, u32[]{:S(2)}, u32[]{:S(2)}) collective-permute-start(bf16[320,1408]{1,0:T(8,128)(2,1)S(1)} %constant_dynamic-slice_fusion.refs_3_), channel_id=1, source_target_pairs={{8,0},{10,2},{16,8},{18,10},{24,16},{26,18},{28,24},{30,26},{20,28... | collective-permute-start | bytes 2703368 | tf_op jit(solution)/shard_map/ppermute | solution.py:133
  27.4 22.0 %collective-permute-start.28 = (bf16[320,1408]{1,0:T(8,128)(2,1)S(1)}, bf16[320,1408]{1,0:T(8,128)(2,1)S(1)}, u32[]{:S(2)}, u32[]{:S(2)}) collective-permute-start(bf16[320,1408]{1,0:T(8,128)(2,1)S(1)} %collective-permute-done.refs_2_), channel_id=1, source_target_pairs={{0,2},{2,0},{4,6},{6,4},{8,10},{10,8},{12,14},{14,12},{16,18},{18,... | collective-permute-start | bytes 2703368 | tf_op jit(solution)/shard_map/ppermute | solution.py:133
  29.5 21.2 %collective-permute-start.30 = (bf16[320,1408]{1,0:T(8,128)(2,1)S(1)}, bf16[320,1408]{1,0:T(8,128)(2,1)S(1)}, u32[]{:S(2)}, u32[]{:S(2)}) collective-permute-start(bf16[320,1408]{1,0:T(8,128)(2,1)S(1)} %collective-permute-done.8.refs_4_), channel_id=1, source_target_pairs={{0,2},{2,0},{4,6},{6,4},{8,10},{10,8},{12,14},{14,12},{16,18},{18,... | collective-permute-start | bytes 2703368 | tf_op jit(solution)/shard_map/ppermute | solution.py:133
  47.4 22.8 %collective-permute-start.1 = (bf16[320,1408]{1,0:T(8,128)(2,1)S(1)}, bf16[320,1408]{1,0:T(8,128)(2,1)S(1)}, u32[]{:S(2)}, u32[]{:S(2)}) collective-permute-start(bf16[320,1408]{1,0:T(8,128)(2,1)S(1)} %collective-permute-done.refs_2_), channel_id=1, source_target_pairs={{0,8},{2,10},{8,16},{10,18},{16,24},{18,26},{24,28},{26,30},{28,20... | collective-permute-start | bytes 2703368 | tf_op jit(solution)/shard_map/ppermute | solution.py:133
  49.3 21.0 %collective-permute-start.31 = (bf16[320,1408]{1,0:T(8,128)(2,1)S(1)}, bf16[320,1408]{1,0:T(8,128)(2,1)S(1)}, u32[]{:S(2)}, u32[]{:S(2)}) collective-permute-start(bf16[320,1408]{1,0:T(8,128)(2,1)S(1)} %collective-permute-done.12.refs_5_), channel_id=1, source_target_pairs={{0,2},{2,0},{4,6},{6,4},{8,10},{10,8},{12,14},{14,12},{16,18},{18,... | collective-permute-start | bytes 2703368 | tf_op jit(solution)/shard_map/ppermute | solution.py:133
  50.5 22.8 %collective-permute-start.9 = (bf16[320,1408]{1,0:T(8,128)(2,1)S(1)}, bf16[320,1408]{1,0:T(8,128)(2,1)S(1)}, u32[]{:S(2)}, u32[]{:S(2)}) collective-permute-start(bf16[320,1408]{1,0:T(8,128)(2,1)S(1)} %collective-permute-done.8.refs_4_), channel_id=1, source_target_pairs={{8,0},{10,2},{16,8},{18,10},{24,16},{26,18},{28,24},{30,26},{20,28... | collective-permute-start | bytes 2703368 | tf_op jit(solution)/shard_map/ppermute | solution.py:133
  50.7 38.9 %collective-permute-start.5 = (bf16[320,1408]{1,0:T(8,128)(2,1)S(1)}, bf16[320,1408]{1,0:T(8,128)(2,1)}, u32[]{:S(2)}, u32[]{:S(2)}) collective-permute-start(bf16[320,1408]{1,0:T(8,128)(2,1)S(1)} %collective-permute-done.4.refs_3_), channel_id=1, source_target_pairs={{0,8},{2,10},{8,16},{10,18},{16,24},{18,26},{24,28},{26,30},{28,20... | collective-permute-start | bytes 2703368 | tf_op jit(solution)/shard_map/ppermute | solution.py:133
  53.5 39.3 %collective-permute-start.13 = (bf16[320,1408]{1,0:T(8,128)(2,1)S(1)}, bf16[320,1408]{1,0:T(8,128)(2,1)}, u32[]{:S(2)}, u32[]{:S(2)}) collective-permute-start(bf16[320,1408]{1,0:T(8,128)(2,1)S(1)} %collective-permute-done.12.refs_5_), channel_id=1, source_target_pairs={{8,0},{10,2},{16,8},{18,10},{24,16},{26,18},{28,24},{30,26},{20,28... | collective-permute-start | bytes 2703368 | tf_op jit(solution)/shard_map/ppermute | solution.py:133
  70.2 24.1 %collective-permute-start.24 = (bf16[320,1408]{1,0:T(8,128)(2,1)S(1)}, bf16[320,1408]{1,0:T(8,128)(2,1)S(1)}, u32[]{:S(2)}, u32[]{:S(2)}) collective-permute-start(bf16[320,1408]{1,0:T(8,128)(2,1)S(1)} %collective-permute-done.1.refs_2_), channel_id=1, source_target_pairs={{0,2},{2,0},{4,6},{6,4},{8,10},{10,8},{12,14},{14,12},{16,18},{18,... | collective-permute-start | bytes 2703368 | tf_op jit(solution)/shard_map/ppermute | solution.py:133
  70.3 38.6 %collective-permute-start.2 = (bf16[320,1408]{1,0:T(8,128)(2,1)S(1)}, bf16[320,1408]{1,0:T(8,128)(2,1)S(1)}, u32[]{:S(2)}, u32[]{:S(2)}) collective-permute-start(bf16[320,1408]{1,0:T(8,128)(2,1)S(1)} %collective-permute-done.1.refs_2_), channel_id=1, source_target_pairs={{0,8},{2,10},{8,16},{10,18},{16,24},{18,26},{24,28},{26,30},{28,20... | collective-permute-start | bytes 2703368 | tf_op jit(solution)/shard_map/ppermute | solution.py:133
  73.3 38.0 %collective-permute-start.10 = (bf16[320,1408]{1,0:T(8,128)(2,1)S(1)}, bf16[320,1408]{1,0:T(8,128)(2,1)S(1)}, u32[]{:S(2)}, u32[]{:S(2)}) collective-permute-start(bf16[320,1408]{1,0:T(8,128)(2,1)S(1)} %collective-permute-done.9.refs_4_), channel_id=1, source_target_pairs={{8,0},{10,2},{16,8},{18,10},{24,16},{26,18},{28,24},{30,26},{20,28... | collective-permute-start | bytes 2703368 | tf_op jit(solution)/shard_map/ppermute | solution.py:133
  89.7 22.0 %collective-permute-start.26 = (bf16[320,1408]{1,0:T(8,128)(2,1)S(1)}, bf16[320,1408]{1,0:T(8,128)(2,1)}, u32[]{:S(2)}, u32[]{:S(2)}) collective-permute-start(bf16[320,1408]{1,0:T(8,128)(2,1)S(1)} %collective-permute-done.9.refs_4_), channel_id=1, source_target_pairs={{0,2},{2,0},{4,6},{6,4},{8,10},{10,8},{12,14},{14,12},{16,18},{18,... | collective-permute-start | bytes 2703368 | tf_op jit(solution)/shard_map/ppermute | solution.py:133
  92.7 35.4 %collective-permute-start.6 = (bf16[320,1408]{1,0:T(8,128)(2,1)}, bf16[320,1408]{1,0:T(8,128)(2,1)S(1)}, u32[]{:S(2)}, u32[]{:S(2)}) collective-permute-start(bf16[320,1408]{1,0:T(8,128)(2,1)} %collective-permute-done.5.refs_3_), channel_id=1, source_target_pairs={{0,8},{2,10},{8,16},{10,18},{16,24},{18,26},{24,28},{26,30},{28,20... | collective-permute-start | bytes 2703368 | tf_op jit(solution)/shard_map/ppermute | solution.py:133
  95.3 44.9 %collective-permute-start.25 = (bf16[320,1408]{1,0:T(8,128)(2,1)}, bf16[320,1408]{1,0:T(8,128)(2,1)}, u32[]{:S(2)}, u32[]{:S(2)}) collective-permute-start(bf16[320,1408]{1,0:T(8,128)(2,1)} %collective-permute-done.5.refs_3_), channel_id=1, source_target_pairs={{0,2},{2,0},{4,6},{6,4},{8,10},{10,8},{12,14},{14,12},{16,18},{18,... | collective-permute-start | bytes 2703368 | tf_op jit(solution)/shard_map/ppermute | solution.py:133
  108.9 31.6 %collective-permute-start.27 = (bf16[320,1408]{1,0:T(8,128)(2,1)}, bf16[320,1408]{1,0:T(8,128)(2,1)}, u32[]{:S(2)}, u32[]{:S(2)}) collective-permute-start(bf16[320,1408]{1,0:T(8,128)(2,1)} %collective-permute-done.13.refs_5_), channel_id=1, source_target_pairs={{0,2},{2,0},{4,6},{6,4},{8,10},{10,8},{12,14},{14,12},{16,18},{18,... | collective-permute-start | bytes 2703368 | tf_op jit(solution)/shard_map/ppermute | solution.py:133
  111.3 29.2 %collective-permute-start.14 = (bf16[320,1408]{1,0:T(8,128)(2,1)}, bf16[320,1408]{1,0:T(8,128)(2,1)S(1)}, u32[]{:S(2)}, u32[]{:S(2)}) collective-permute-start(bf16[320,1408]{1,0:T(8,128)(2,1)} %collective-permute-done.13.refs_5_), channel_id=1, source_target_pairs={{8,0},{10,2},{16,8},{18,10},{24,16},{26,18},{28,24},{30,26},{20,28... | collective-permute-start | bytes 2703368 | tf_op jit(solution)/shard_map/ppermute | solution.py:133
  111.7 29.3 %collective-permute-start.3 = (bf16[160,1408]{1,0:T(8,128)(2,1)S(1)}, bf16[160,1408]{1,0:T(8,128)(2,1)S(1)}, u32[]{:S(2)}, u32[]{:S(2)}) collective-permute-start(bf16[160,1408]{1,0:T(8,128)(2,1)S(1)} %slice.16), channel_id=1, source_target_pairs={{0,8},{2,10},{8,16},{10,18},{16,24},{18,26},{24,28},{26,30},{28,20... | collective-permute-start | bytes 1351688 | tf_op jit(solution)/shard_map/ppermute | solution.py:133
  128.2 14.4 %collective-permute-start.11 = (bf16[160,1408]{1,0:T(8,128)(2,1)S(1)}, bf16[160,1408]{1,0:T(8,128)(2,1)S(1)}, u32[]{:S(2)}, u32[]{:S(2)}) collective-permute-start(bf16[160,1408]{1,0:T(8,128)(2,1)S(1)} %slice.18), channel_id=1, source_target_pairs={{8,0},{10,2},{16,8},{18,10},{24,16},{26,18},{28,24},{30,26},{20,28... | collective-permute-start | bytes 1351688 | tf_op jit(solution)/shard_map/ppermute | solution.py:133
  140.2 17.9 %collective-permute-start.7 = (bf16[160,1408]{1,0:T(8,128)(2,1)S(1)}, bf16[160,1408]{1,0:T(8,128)(2,1)S(1)}, u32[]{:S(2)}, u32[]{:S(2)}) collective-permute-start(bf16[160,1408]{1,0:T(8,128)(2,1)S(1)} %slice.17), channel_id=1, source_target_pairs={{0,8},{2,10},{8,16},{10,18},{16,24},{18,26},{24,28},{26,30},{28,20... | collective-permute-start | bytes 1351688 | tf_op jit(solution)/shard_map/ppermute | solution.py:133
  140.5 33.3 %collective-permute-start.20 = (bf16[320,1408]{1,0:T(8,128)(2,1)S(1)}, bf16[320,1408]{1,0:T(8,128)(2,1)S(1)}, u32[]{:S(2)}, u32[]{:S(2)}) collective-permute-start(bf16[320,1408]{1,0:T(8,128)(2,1)S(1)} %collective-permute-done.2.refs_2_), channel_id=1, source_target_pairs={{0,2},{2,0},{4,6},{6,4},{8,10},{10,8},{12,14},{14,12},{16,18},{18,... | collective-permute-start | bytes 2703368 | tf_op jit(solution)/shard_map/ppermute | solution.py:133
  140.5 33.8 %collective-permute-start.22 = (bf16[320,1408]{1,0:T(8,128)(2,1)S(1)}, bf16[320,1408]{1,0:T(8,128)(2,1)}, u32[]{:S(2)}, u32[]{:S(2)}) collective-permute-start(bf16[320,1408]{1,0:T(8,128)(2,1)S(1)} %collective-permute-done.10.refs_4_), channel_id=1, source_target_pairs={{0,2},{2,0},{4,6},{6,4},{8,10},{10,8},{12,14},{14,12},{16,18},{18,... | collective-permute-start | bytes 2703368 | tf_op jit(solution)/shard_map/ppermute | solution.py:133
  141.0 33.4 %collective-permute-start.21 = (bf16[320,1408]{1,0:T(8,128)(2,1)S(1)}, bf16[320,1408]{1,0:T(8,128)(2,1)}, u32[]{:S(2)}, u32[]{:S(2)}) collective-permute-start(bf16[320,1408]{1,0:T(8,128)(2,1)S(1)} %collective-permute-done.6.refs_3_), channel_id=1, source_target_pairs={{0,2},{2,0},{4,6},{6,4},{8,10},{10,8},{12,14},{14,12},{16,18},{18,... | collective-permute-start | bytes 2703368 | tf_op jit(solution)/shard_map/ppermute | solution.py:133
  142.5 32.3 %collective-permute-start.23 = (bf16[320,1408]{1,0:T(8,128)(2,1)S(1)}, bf16[320,1408]{1,0:T(8,128)(2,1)}, u32[]{:S(2)}, u32[]{:S(2)}) collective-permute-start(bf16[320,1408]{1,0:T(8,128)(2,1)S(1)} %collective-permute-done.14.refs_5_), channel_id=1, source_target_pairs={{0,2},{2,0},{4,6},{6,4},{8,10},{10,8},{12,14},{14,12},{16,18},{18,... | collective-permute-start | bytes 2703368 | tf_op jit(solution)/shard_map/ppermute | solution.py:133
  158.1 15.7 %collective-permute-start.15 = (bf16[160,1408]{1,0:T(8,128)(2,1)S(1)}, bf16[160,1408]{1,0:T(8,128)(2,1)S(1)}, u32[]{:S(2)}, u32[]{:S(2)}) collective-permute-start(bf16[160,1408]{1,0:T(8,128)(2,1)S(1)} %slice.19), channel_id=1, source_target_pairs={{8,0},{10,2},{16,8},{18,10},{24,16},{26,18},{28,24},{30,26},{20,28... | collective-permute-start | bytes 1351688 | tf_op jit(solution)/shard_map/ppermute | solution.py:133
  173.8 14.1 %collective-permute-start.16 = (bf16[160,1408]{1,0:T(8,128)(2,1)S(1)}, bf16[160,1408]{1,0:T(8,128)(2,1)S(1)}, u32[]{:S(2)}, u32[]{:S(2)}) collective-permute-start(bf16[160,1408]{1,0:T(8,128)(2,1)S(1)} %collective-permute-done.3.refs_2_), channel_id=1, source_target_pairs={{0,2},{2,0},{4,6},{6,4},{8,10},{10,8},{12,14},{14,12},{16,18},{18,... | collective-permute-start | bytes 1351688 | tf_op jit(solution)/shard_map/ppermute | solution.py:133
  173.8 14.1 %collective-permute-start.18 = (bf16[160,1408]{1,0:T(8,128)(2,1)S(1)}, bf16[160,1408]{1,0:T(8,128)(2,1)S(1)}, u32[]{:S(2)}, u32[]{:S(2)}) collective-permute-start(bf16[160,1408]{1,0:T(8,128)(2,1)S(1)} %collective-permute-done.11.refs_4_), channel_id=1, source_target_pairs={{0,2},{2,0},{4,6},{6,4},{8,10},{10,8},{12,14},{14,12},{16,18},{18,... | collective-permute-start | bytes 1351688 | tf_op jit(solution)/shard_map/ppermute | solution.py:133
  174.3 13.6 %collective-permute-start.17 = (bf16[160,1408]{1,0:T(8,128)(2,1)S(1)}, bf16[160,1408]{1,0:T(8,128)(2,1)S(1)}, u32[]{:S(2)}, u32[]{:S(2)}) collective-permute-start(bf16[160,1408]{1,0:T(8,128)(2,1)S(1)} %collective-permute-done.7.refs_3_), channel_id=1, source_target_pairs={{0,2},{2,0},{4,6},{6,4},{8,10},{10,8},{12,14},{14,12},{16,18},{18,... | collective-permute-start | bytes 1351688 | tf_op jit(solution)/shard_map/ppermute | solution.py:133
  196.4 41.4 %collective-permute-start.34 = (bf16[640,1408]{1,0:T(8,128)(2,1)S(1)}, bf16[640,1408]{1,0:T(8,128)(2,1)S(1)}, u32[]{:S(2)}, u32[]{:S(2)}) collective-permute-start(bf16[640,1408]{1,0:T(8,128)(2,1)S(1)} %shard_map.32), channel_id=1, source_target_pairs={{0,1},{1,0},{2,3},{3,2},{4,5},{5,4},{6,7},{7,6},{8,9},{9,8},{10,11... | collective-permute-start | bytes 5406728 | tf_op jit(solution)/shard_map/ppermute | solution.py:98
  (25 other events, 478.0 us)
where the time goes:
time: 241 us; the launch traced here: 240 us
  waiting for transfers between devices  142 us (59%)
  Pallas kernels  55.9 us (23%)
  starting transfers between devices  21.7 us (9%)
  local copies, waits for them, and re-layouts  12.7 us (5%)
  other arithmetic  7.71 us (3%)
    ppermute x34, waiting for transfers between devices, send(): return tuple((lax.ppermute(part, 'seq', route) for part in parts))  102 us
    pallas_call x5, Pallas kernels, add_relation(): pl.pallas_call(functools.partial(relation_kernel, margin, weight, counts,...  55.9 us
    ppermute x1, waiting for transfers between devices, sum_over_pair(): lax.ppermute(half, 'pair', [(i, i ^ distance) for i in range(count)])  39.8 us
    ppermute x34, starting transfers between devices, send(): return tuple((lax.ppermute(part, 'seq', route) for part in parts))  20.1 us
    unnamed x44, local copies, waits for them, and re-layouts  12.2 us
  transfers between devices with their start and end apart: 35, of which 12 were waited for; matrix products, arithmetic and copies ran while one was open for 1% of the time, Pallas kernels for 20%

commit v1 on v0

v1 whole, which is shorter than its diff:
```python
import functools
import math

import jax
import jax.numpy as jnp
from jax import lax
from jax.experimental import pallas as pl
from jax.experimental.pallas import tpu as pltpu
from jax.sharding import PartitionSpec as P

CORES = 2
ROW_TILE = 16
VMEM_LIMIT = 32 * 1024 * 1024


def normalize(values, width):
    scale = lax.rsqrt(jnp.sum(values * values, axis=1, keepdims=True) + width * 1e-06)
    return (scale, values * scale)


def relation_kernel(margin, weight, counts, has_total, project, *refs):
    refs = list(refs)
    own_s, own_t = refs[:2]
    partners = refs[2 : 2 + len(counts)]
    rest = refs[2 + len(counts) :]
    total = rest.pop(0) if has_total else None
    student, scale = (rest.pop(0), rest.pop(0)) if project else (None, None)
    out, all_s, all_t = rest

    @pl.when(pl.program_id(0) == 0)
    def _():
        at = 0
        for partner, count in zip(partners, counts):
            all_s[at : at + count, :] = partner[:count, :]
            all_t[at : at + count, :] = partner[count:, :]
            at += count

    contract = (((1,), (1,)), ((), ()))
    s_rel = lax.dot_general(own_s[...], all_s[...], contract, preferred_element_type=jnp.float32)
    t_rel = lax.dot_general(own_t[...], all_t[...], contract, preferred_element_type=jnp.float32)
    delta = s_rel - t_rel
    shrink = jnp.maximum(delta - margin, 0.0) + jnp.minimum(delta + margin, 0.0)
    relation = (weight * shrink).astype(jnp.bfloat16)
    grad = jnp.dot(relation, all_s[...], preferred_element_type=jnp.float32)
    if has_total:
        grad = total[...] + grad
    if project:
        unit = student[...] * scale[...]
        grad = grad - unit * jnp.sum(unit * grad, axis=1, keepdims=True)
    out[...] = grad.astype(out.dtype)


def add_relation(own, partners, total, margin, weight, project=None, dtype=jnp.float32):
    rows, width = own[0].shape
    block = rows // 2
    counts = tuple(x.shape[0] // 2 for x in partners)
    tokens = sum(counts)
    by_row = pl.BlockSpec((block, width), lambda i: (i, 0))
    operands = list(own) + list(partners)
    specs = [by_row, by_row] + [
        pl.BlockSpec(x.shape, lambda i: (0, 0), pipeline_mode=pl.Buffered(1)) for x in partners
    ]
    aliases = {}
    if total is not None:
        if dtype == total.dtype:
            aliases = {len(operands): 0}
        operands.append(total)
        specs.append(by_row)
    if project is not None:
        operands += list(project)
        specs += [by_row, pl.BlockSpec((block, 1), lambda i: (i, 0))]
    return pl.pallas_call(
        functools.partial(
            relation_kernel, margin, weight, counts, total is not None, project is not None
        ),
        grid=(rows // block,),
        in_specs=specs,
        out_specs=by_row,
        out_shape=jax.ShapeDtypeStruct((rows, width), dtype),
        scratch_shapes=[pltpu.VMEM((tokens, width), jnp.bfloat16)] * 2,
        input_output_aliases=aliases,
        compiler_params=pltpu.CompilerParams(vmem_limit_bytes=VMEM_LIMIT),
        cost_estimate=pl.CostEstimate(
            flops=6 * rows * tokens * width,
            bytes_accessed=4 * rows * width + 4 * tokens * width + 8 * rows * width,
            transcendentals=0,
        ),
    )(*operands)


def ring_routes(count):
    chips = count // CORES
    order = list(range(0, chips, 2)) + list(range(1, chips, 2))[::-1]
    onward, back = [], []
    for place, chip in enumerate(order):
        following = order[(place + 1) % chips]
        for core in range(CORES):
            onward.append((chip * CORES + core, following * CORES + core))
            back.append((following * CORES + core, chip * CORES + core))
    swap = [(i, i ^ 1) for i in range(count)]
    return onward, back, swap


def halves(tokens):
    first = -(-tokens // (2 * ROW_TILE)) * ROW_TILE
    return first, tokens - first


def local(student, teacher):
    rows, width = student.shape
    seq_count = lax.axis_size("seq")
    pair_count = lax.axis_size("pair")
    pair_index = lax.axis_index("pair")
    margin = 0.75 / math.sqrt(width)
    weight = 64.0 * width / math.sqrt(rows * seq_count)
    s_scale, s_unit = normalize(student, width)
    t_scale, t_unit = normalize(teacher, width)
    s_half = s_unit.astype(jnp.bfloat16)
    t_half = t_unit.astype(jnp.bfloat16)
    share = rows // pair_count
    onward, back, swap = ring_routes(seq_count)
    hops = seq_count // CORES // 2

    def send(groups):
        return [(way, [lax.ppermute(x, "seq", way) for x in xs]) for way, xs in groups]

    def swapped(groups):
        return [lax.ppermute(x, "seq", swap) for _, xs in groups for x in xs]

    def arrays(groups):
        return [x for _, xs in groups for x in xs]

    def after(groups, value):
        return [(way, [lax.optimization_barrier((x, value))[0] for x in xs]) for way, xs in groups]

    def add(partners, total, project=None, dtype=jnp.float32):
        return add_relation((s_half, t_half), partners, total, margin, weight, project, dtype)

    def add_groups(groups, total, project=None, dtype=jnp.float32):
        return add(arrays(groups) + swapped(groups), total, project, dtype)

    def piece(start, count):
        at = pair_index * share + start
        cut = lambda x: lax.dynamic_slice_in_dim(x, at, count, 0)
        return jnp.concatenate([cut(s_half), cut(t_half)])

    first, second = halves(share)
    own = [piece(0, first), piece(first, second)]

    def in_two(x):
        tokens = x.shape[0] // 2
        left, right = halves(tokens)
        cut = lambda at, count: jnp.concatenate([x[at : at + count], x[tokens + at : tokens + at + count]])
        return [cut(0, left), cut(left, right)]

    far = [(onward, in_two(own[0])), (back, in_two(own[1]))]
    near = [(onward, [own[1]]), (back, [own[0]])]
    waiting = [(onward, own)]
    total = None
    far = send(far)
    for hop in range(2, hops):
        total = add_groups(waiting, total)
        waiting = far
        if hop == hops - 1:
            near = after(after(near, total), far[0][1][0])
        far = send(after(far, total))
    near = send(near)
    total = add_groups(waiting, total)
    mine = after(far, total)
    theirs = [
        [
            (way, [lax.ppermute(x, "pair", [(i, (i + k) % pair_count) for i in range(pair_count)]) for x in xs])
            for way, xs in mine
        ]
        for k in range(1, pair_count)
    ]
    waiting = far
    for hop in range(2, hops):
        following = send(after(near, total))
        total = add_groups(waiting, total)
        waiting = near
        near = following
    last = after(send(after(mine, near[0][1][0])), total)
    total = add_groups(waiting, total)
    partial_grad = add_groups(near, total, (student, s_scale), jnp.bfloat16)
    summed = partial_grad.astype(jnp.float32)
    distance = 1
    while distance < pair_count:
        half = summed.astype(jnp.bfloat16)
        other = lax.ppermute(half, "pair", [(i, i ^ distance) for i in range(pair_count)])
        summed = half.astype(jnp.float32) + other.astype(jnp.float32)
        distance *= 2
    rest = [send(after(groups, partial_grad)) for groups in theirs]
    total = add_groups(last, None)
    for k, groups in enumerate(rest):
        final = (student, s_scale) if k == len(rest) - 1 else None
        total = add_groups(groups, total, final)
    return s_scale * (summed + total)


def solution(mesh):
    placed = (P("seq", None), P("seq", None))
    return jax.shard_map(
        local, mesh=mesh, in_specs=placed, out_specs=P("seq", None), check_vma=False
    )
```

time: 241 us -> 261 us (1.083)
  starting transfers between devices: 21.7 us -> 39.7 us
  waiting for transfers between devices: 142 us -> 157 us
  local copies, waits for them, and re-layouts: 12.7 us -> 4.93 us
  Pallas kernels: 55.9 us -> 50.8 us
    ppermute x35 -> x59, starting transfers between devices: 21.7 us -> 39.7 us  [the longest x26 29.9 us: send(): lax.ppermute(x, 'seq', way)]
    ppermute x35 -> x59, waiting for transfers between devices: 142 us -> 157 us  [the longest x26 128 us: send(): lax.ppermute(x, 'seq', way)]
    unnamed x44 -> x8, local copies, waits for them, and re-layouts: 12.2 us -> 1.9 us
    pallas_call x5 -> x9, Pallas kernels: 55.9 us -> 50.8 us  [add_relation(): pl.pallas_call(functools.partial(relation_kernel, margin, weight, counts,...]
  transfers between devices with their start and end apart: 35 -> 59, of which waited for: 12 -> 26; matrix products, arithmetic and copies ran while one was open for 1% -> 1% of each run, Pallas kernels for 20% -> 19%
where the time goes in v1:
time: 261 us
  waiting for transfers between devices  157 us (60%)
  Pallas kernels  50.8 us (19%)
  starting transfers between devices  39.7 us (15%)
  other arithmetic  8.3 us (3%)
  local copies, waits for them, and re-layouts  4.93 us (2%)
    ppermute x26, waiting for transfers between devices, send(): lax.ppermute(x, 'seq', way)  128 us
    pallas_call x9, Pallas kernels, add_relation(): pl.pallas_call(functools.partial(relation_kernel, margin, weight, counts,...  50.8 us
    ppermute x26, starting transfers between devices, send(): lax.ppermute(x, 'seq', way)  29.9 us
    ppermute x4, waiting for transfers between devices, local(): lax.ppermute(x, 'pair', [(i, (i + k) % pair_count) for i in range(pair_co...  25.3 us
  transfers between devices with their start and end apart: 59, of which 26 were waited for; matrix products, arithmetic and copies ran while one was open for 1% of the time, Pallas kernels for 19%

profile of v1, /device:TPU:0, one launch (start us, length us, event | category | flops | bytes accessed | tf_op | source)
XLA Modules:
  0.0 260.8 jit_solution(5005471722298566921)
XLA Ops:
  0.0 2.5 multiply_reduce_fusion.1
  11.1 3.1 %collective-permute-start = (bf16[160,1408]{1,0:T(8,128)(2,1)S(1)}, bf16[160,1408]{1,0:T(8,128)(2,1)S(1)}, u32[]{:S(2)}, u32[]{:S(2)}) collective-permute-start(bf16[160,1408]{1,0:T(8,128)(2,1)S(1)} %pad_maximum_fusion.2), channel_id=1, source_target_pairs={{0,8},{2,10},{8,16},{10,18},{16,24},{18,26},{24,28},{26,30},{28,20... | collective-permute-start | bytes 1351688 | tf_op jit(solution)/shard_map/ppermute | solution.py:125
  16.4 8.8 %collective-permute-done.refs_2_ = bf16[160,1408]{1,0:T(8,128)(2,1)S(1)} collective-permute-done((bf16[160,1408]{1,0:T(8,128)(2,1)S(1)}, bf16[160,1408]{1,0:T(8,128)(2,1)S(1)}, u32[]{:S(2)}, u32[]{:S(2)}) %collective-permute-start) | collective-permute-done | bytes 450592 | tf_op jit(solution)/shard_map/ppermute | solution.py:125
  27.3 7.0 %collective-permute-done.1.refs_3_ = bf16[160,1408]{1,0:T(8,128)(2,1)S(1)} collective-permute-done((bf16[160,1408]{1,0:T(8,128)(2,1)S(1)}, bf16[160,1408]{1,0:T(8,128)(2,1)S(1)}, u32[]{:S(2)}, u32[]{:S(2)}) %collective-permute-start.1) | collective-permute-done | bytes 450592 | tf_op jit(solution)/shard_map/ppermute | solution.py:125
  34.8 2.5 collective-permute-done.3.refs_5_
  37.8 6.9 %shard_map.28.refs_10_ = f32[640,1408]{1,0:T(8,128)S(1)} custom-call(bf16[640,1408]{1,0:T(8,128)(2,1)S(1)} %multiply_convert_fusion.1.refs_0_, bf16[640,1408]{1,0:T(8,128)(2,1)S(1)} %copy-done, bf16[320,1408]{1,0:T(8,128)(2,1)S(1)} %pad_maximum_fusion.1.refs_2_, bf16[320,1408]{1,0:T(8,128)(2,1)} %pad_maximum_fusion.refs_3_, ...), custom_call_target="tpu_custom_call" | custom-call | flops 3460300800 | bytes 14417920 | tf_op jit(solution)/shard_map/pallas_call | solution.py:72
  48.4 5.4 %shard_map.29.refs_10_ = f32[640,1408]{1,0:T(8,128)S(1)} custom-call(bf16[640,1408]{1,0:T(8,128)(2,1)S(1)} %multiply_convert_fusion.1.refs_0_, bf16[640,1408]{1,0:T(8,128)(2,1)S(1)} %copy-done, bf16[160,1408]{1,0:T(8,128)(2,1)S(1)} %collective-permute-done.refs_2_, ...), custom_call_target="tpu_custom_call", output_to_operand_aliasing={{}: (10, {})} | custom-call | flops 3460300800 | bytes 14417920 | tf_op jit(solution)/shard_map/pallas_call | solution.py:72
  54.3 3.7 %collective-permute-done.10.refs_2_ = bf16[160,1408]{1,0:T(8,128)(2,1)S(1)} collective-permute-done((bf16[160,1408]{1,0:T(8,128)(2,1)S(1)}, bf16[160,1408]{1,0:T(8,128)(2,1)S(1)}, u32[]{:S(2)}, u32[]{:S(2)}) %collective-permute-start.10) | collective-permute-done | bytes 450592 | tf_op jit(solution)/shard_map/ppermute | solution.py:125
  59.6 8.1 %collective-permute-done.12.refs_3_ = bf16[160,1408]{1,0:T(8,128)(2,1)S(1)} collective-permute-done((bf16[160,1408]{1,0:T(8,128)(2,1)S(1)}, bf16[160,1408]{1,0:T(8,128)(2,1)S(1)}, u32[]{:S(2)}, u32[]{:S(2)}) %collective-permute-start.12) | collective-permute-done | bytes 450592 | tf_op jit(solution)/shard_map/ppermute | solution.py:125
  73.3 13.6 %collective-permute-done.11.refs_2_ = bf16[320,1408]{1,0:T(8,128)(2,1)S(1)} collective-permute-done((bf16[320,1408]{1,0:T(8,128)(2,1)}, bf16[320,1408]{1,0:T(8,128)(2,1)S(1)}, u32[]{:S(2)}, u32[]{:S(2)}) %collective-permute-start.11) | collective-permute-done | bytes 901152 | tf_op jit(solution)/shard_map/ppermute | solution.py:125
  87.5 5.4 %shard_map.30.refs_10_ = f32[640,1408]{1,0:T(8,128)S(1)} custom-call(bf16[640,1408]{1,0:T(8,128)(2,1)S(1)} %multiply_convert_fusion.1.refs_0_, bf16[640,1408]{1,0:T(8,128)(2,1)S(1)} %copy-done, bf16[160,1408]{1,0:T(8,128)(2,1)S(1)} %collective-permute-done.10.refs_2_, ...), custom_call_target="tpu_custom_call", output_to_operand_aliasing={{}: (10, {})} | custom-call | flops 3460300800 | bytes 14417920 | tf_op jit(solution)/shard_map/pallas_call | solution.py:72
  92.9 3.7 %collective-permute-done.21.refs_3_ = bf16[160,1408]{1,0:T(8,128)(2,1)S(1)} collective-permute-done((bf16[160,1408]{1,0:T(8,128)(2,1)S(1)}, bf16[160,1408]{1,0:T(8,128)(2,1)S(1)}, u32[]{:S(2)}, u32[]{:S(2)}) %collective-permute-start.21) | collective-permute-done | bytes 450592 | tf_op jit(solution)/shard_map/ppermute | solution.py:125
  98.2 8.1 %collective-permute-done.20.refs_2_ = bf16[160,1408]{1,0:T(8,128)(2,1)S(1)} collective-permute-done((bf16[160,1408]{1,0:T(8,128)(2,1)S(1)}, bf16[160,1408]{1,0:T(8,128)(2,1)S(1)}, u32[]{:S(2)}, u32[]{:S(2)}) %collective-permute-start.20) | collective-permute-done | bytes 450592 | tf_op jit(solution)/shard_map/ppermute | solution.py:125
  106.8 4.2 %collective-permute-done.23.refs_5_ = bf16[160,1408]{1,0:T(8,128)(2,1)S(1)} collective-permute-done((bf16[160,1408]{1,0:T(8,128)(2,1)S(1)}, bf16[160,1408]{1,0:T(8,128)(2,1)S(1)}, u32[]{:S(2)}, u32[]{:S(2)}) %collective-permute-start.23) | collective-permute-done | bytes 450592 | tf_op jit(solution)/shard_map/ppermute | solution.py:125
  113.5 5.4 %shard_map.31.refs_6_ = f32[640,1408]{1,0:T(8,128)S(1)} custom-call(bf16[640,1408]{1,0:T(8,128)(2,1)S(1)} %multiply_convert_fusion.1.refs_0_, bf16[640,1408]{1,0:T(8,128)(2,1)S(1)} %copy-done, bf16[160,1408]{1,0:T(8,128)(2,1)S(1)} %collective-permute-done.20.refs_2_, ...), custom_call_target="tpu_custom_call", output_to_operand_aliasing={{}: (10, {})} | custom-call | flops 3460300800 | bytes 14417920 | tf_op jit(solution)/shard_map/pallas_call | solution.py:72
  118.8 5.8 %collective-permute-done.19.refs_2_ = bf16[320,1408]{1,0:T(8,128)(2,1)S(1)} collective-permute-done((bf16[320,1408]{1,0:T(8,128)(2,1)S(1)}, bf16[320,1408]{1,0:T(8,128)(2,1)S(1)}, u32[]{:S(2)}, u32[]{:S(2)}) %collective-permute-start.19) | collective-permute-done | bytes 901152 | tf_op jit(solution)/shard_map/ppermute | solution.py:125
  126.8 6.9 %collective-permute-done.30.refs_3_ = bf16[320,1408]{1,0:T(8,128)(2,1)S(1)} collective-permute-done((bf16[320,1408]{1,0:T(8,128)(2,1)S(1)}, bf16[320,1408]{1,0:T(8,128)(2,1)S(1)}, u32[]{:S(2)}, u32[]{:S(2)}) %collective-permute-start.30) | collective-permute-done | bytes 901152 | tf_op jit(solution)/shard_map/ppermute | solution.py:125
  134.2 11.6 %collective-permute-done.28.refs_2_ = bf16[320,1408]{1,0:T(8,128)(2,1)S(1)} collective-permute-done((bf16[320,1408]{1,0:T(8,128)(2,1)S(1)}, bf16[320,1408]{1,0:T(8,128)(2,1)S(1)}, u32[]{:S(2)}, u32[]{:S(2)}) %collective-permute-start.28) | collective-permute-done | bytes 901152 | tf_op jit(solution)/shard_map/ppermute | solution.py:125
  149.4 7.2 %collective-permute-done.31.refs_3_ = bf16[320,1408]{1,0:T(8,128)(2,1)S(1)} collective-permute-done((bf16[320,1408]{1,0:T(8,128)(2,1)S(1)}, bf16[320,1408]{1,0:T(8,128)(2,1)S(1)}, u32[]{:S(2)}, u32[]{:S(2)}) %collective-permute-start.31) | collective-permute-done | bytes 901152 | tf_op jit(solution)/shard_map/ppermute | solution.py:125
  159.0 6.9 %collective-permute-done.52.refs_3_ = bf16[160,1408]{1,0:T(8,128)(2,1)S(1)} collective-permute-done((bf16[160,1408]{1,0:T(8,128)(2,1)S(1)}, bf16[160,1408]{1,0:T(8,128)(2,1)S(1)}, u32[]{:S(2)}, u32[]{:S(2)}) %collective-permute-start.52) | collective-permute-done | bytes 450592 | tf_op jit(solution)/shard_map/ppermute | solution.py:125
  166.6 5.4 %shard_map.32.refs_6_ = f32[640,1408]{1,0:T(8,128)S(1)} custom-call(bf16[640,1408]{1,0:T(8,128)(2,1)S(1)} %multiply_convert_fusion.1.refs_0_, bf16[640,1408]{1,0:T(8,128)(2,1)S(1)} %copy-done, bf16[320,1408]{1,0:T(8,128)(2,1)S(1)} %collective-permute-done.11.refs_2_, ...), custom_call_target="tpu_custom_call", output_to_operand_aliasing={{}: (6, {})} | custom-call | flops 3460300800 | bytes 14417920 | tf_op jit(solution)/shard_map/pallas_call | solution.py:72
  172.0 6.7 %collective-permute-done.54.refs_5_ = bf16[160,1408]{1,0:T(8,128)(2,1)S(1)} collective-permute-done((bf16[160,1408]{1,0:T(8,128)(2,1)S(1)}, bf16[160,1408]{1,0:T(8,128)(2,1)S(1)}, u32[]{:S(2)}, u32[]{:S(2)}) %collective-permute-start.54) | collective-permute-done | bytes 450592 | tf_op jit(solution)/shard_map/ppermute | solution.py:125
  182.8 5.4 %shard_map.33.refs_6_ = f32[640,1408]{1,0:T(8,128)S(1)} custom-call(bf16[640,1408]{1,0:T(8,128)(2,1)S(1)} %multiply_convert_fusion.1.refs_0_, bf16[640,1408]{1,0:T(8,128)(2,1)S(1)} %copy-done, bf16[320,1408]{1,0:T(8,128)(2,1)S(1)} %collective-permute-done.19.refs_2_, ...), custom_call_target="tpu_custom_call", output_to_operand_aliasing={{}: (6, {})} | custom-call | flops 3460300800 | bytes 14417920 | tf_op jit(solution)/shard_map/pallas_call | solution.py:72
  188.2 5.9 %shard_map.34 = bf16[640,1408]{1,0:T(8,128)(2,1)S(1)} custom-call(bf16[640,1408]{1,0:T(8,128)(2,1)S(1)} %multiply_convert_fusion.1.refs_0_, bf16[640,1408]{1,0:T(8,128)(2,1)S(1)} %copy-done, bf16[320,1408]{1,0:T(8,128)(2,1)S(1)} %collective-permute-done.28.refs_2_, bf16[320,1408]{1,0:T(8,128)(2,1)S(1)} %collective-permute-done.31.refs_3_, ...), custom_call_target="tpu_custom_call" | custom-call | flops 3460300800 | bytes 14417920 | tf_op jit(solution)/shard_map/pallas_call | solution.py:72
  195.6 6.0 %collective-permute-done.43 = bf16[160,1408]{1,0:T(8,128)(2,1)S(1)} collective-permute-done((bf16[160,1408]{1,0:T(8,128)(2,1)S(1)}, bf16[160,1408]{1,0:T(8,128)(2,1)S(1)}, u32[]{:S(2)}, u32[]{:S(2)}) %collective-permute-start.43) | collective-permute-done | bytes 450592 | tf_op jit(solution)/shard_map/ppermute | solution.py:172
  201.6 9.7 %collective-permute-done.41 = bf16[160,1408]{1,0:T(8,128)(2,1)S(1)} collective-permute-done((bf16[160,1408]{1,0:T(8,128)(2,1)S(1)}, bf16[160,1408]{1,0:T(8,128)(2,1)S(1)}, u32[]{:S(2)}, u32[]{:S(2)}) %collective-permute-start.41) | collective-permute-done | bytes 450592 | tf_op jit(solution)/shard_map/ppermute | solution.py:172
  211.3 9.7 %collective-permute-done.39 = bf16[160,1408]{1,0:T(8,128)(2,1)S(1)} collective-permute-done((bf16[160,1408]{1,0:T(8,128)(2,1)S(1)}, bf16[160,1408]{1,0:T(8,128)(2,1)S(1)}, u32[]{:S(2)}, u32[]{:S(2)}) %collective-permute-start.39) | collective-permute-done | bytes 450592 | tf_op jit(solution)/shard_map/ppermute | solution.py:172
  225.0 9.1 %collective-permute-done.46.refs_5_ = bf16[160,1408]{1,0:T(8,128)(2,1)S(1)} collective-permute-done((bf16[160,1408]{1,0:T(8,128)(2,1)S(1)}, bf16[160,1408]{1,0:T(8,128)(2,1)S(1)}, u32[]{:S(2)}, u32[]{:S(2)}) %collective-permute-start.46) | collective-permute-done | bytes 450592 | tf_op jit(solution)/shard_map/ppermute | solution.py:125
  234.1 9.3 %collective-permute-done.44.refs_4_ = bf16[160,1408]{1,0:T(8,128)(2,1)S(1)} collective-permute-done((bf16[160,1408]{1,0:T(8,128)(2,1)S(1)}, bf16[160,1408]{1,0:T(8,128)(2,1)S(1)}, u32[]{:S(2)}, u32[]{:S(2)}) %collective-permute-start.44) | collective-permute-done | bytes 450592 | tf_op jit(solution)/shard_map/ppermute | solution.py:125
  244.9 5.2 %shard_map.35.refs_10_ = f32[640,1408]{1,0:T(8,128)S(1)} custom-call(bf16[640,1408]{1,0:T(8,128)(2,1)S(1)} %multiply_convert_fusion.1.refs_0_, bf16[640,1408]{1,0:T(8,128)(2,1)S(1)} %copy-done, bf16[160,1408]{1,0:T(8,128)(2,1)S(1)} %collective-permute-done.51.refs_2_, bf16[160,1408]{1,0:T(8,128)(2,1)S(1)} %collective-permute-done.52.refs_3_, ...), custom_call_target="tpu_custom_call" | custom-call | flops 3460300800 | bytes 14417920 | tf_op jit(solution)/shard_map/pallas_call | solution.py:72
  250.1 5.9 %shard_map.36 = f32[640,1408]{1,0:T(8,128)S(1)} custom-call(bf16[640,1408]{1,0:T(8,128)(2,1)S(1)} %multiply_convert_fusion.1.refs_0_, bf16[640,1408]{1,0:T(8,128)(2,1)S(1)} %copy-done, bf16[160,1408]{1,0:T(8,128)(2,1)S(1)} %collective-permute-done.40.refs_2_, bf16[160,1408]{1,0:T(8,128)(2,1)S(1)} %collective-permute-done.42.refs_3_, ...), custom_call_target="tpu_custom_call", output_to_operand_aliasing={{}: (10, {})} | custom-call | flops 3460300800 | bytes 14417920 | tf_op jit(solution)/shard_map/pallas_call | solution.py:72
  258.3 2.5 add_multiply_fusion
  (119 shorter events, 53.2 us)
Async XLA Ops:
  8.8 28.5 %collective-permute-start.9 = (bf16[320,1408]{1,0:T(8,128)(2,1)}, bf16[320,1408]{1,0:T(8,128)(2,1)}, u32[]{:S(2)}, u32[]{:S(2)}) collective-permute-start(bf16[320,1408]{1,0:T(8,128)(2,1)} %pad_maximum_fusion.refs_3_), channel_id=1, source_target_pairs={{0,2},{2,0},{4,6},{6,4},{8,10},{10,8},{12,14},{14,12},{16,18},{18,... | collective-permute-start | bytes 2703368 | tf_op jit(solution)/shard_map/ppermute | solution.py:128
  9.3 28.5 %collective-permute-start.8 = (bf16[320,1408]{1,0:T(8,128)(2,1)S(1)}, bf16[320,1408]{1,0:T(8,128)(2,1)}, u32[]{:S(2)}, u32[]{:S(2)}) collective-permute-start(bf16[320,1408]{1,0:T(8,128)(2,1)S(1)} %pad_maximum_fusion.1.refs_2_), channel_id=1, source_target_pairs={{0,2},{2,0},{4,6},{6,4},{8,10},{10,8},{12,14},{14,12},{16,18},{18,... | collective-permute-start | bytes 2703368 | tf_op jit(solution)/shard_map/ppermute | solution.py:128
  14.2 20.1 %collective-permute-start.1 = (bf16[160,1408]{1,0:T(8,128)(2,1)S(1)}, bf16[160,1408]{1,0:T(8,128)(2,1)S(1)}, u32[]{:S(2)}, u32[]{:S(2)}) collective-permute-start(bf16[160,1408]{1,0:T(8,128)(2,1)S(1)} %pad_maximum_fusion.3), channel_id=1, source_target_pairs={{0,8},{2,10},{8,16},{10,18},{16,24},{18,26},{24,28},{26,30},{28,20... | collective-permute-start | bytes 1351688 | tf_op jit(solution)/shard_map/ppermute | solution.py:125
  15.9 18.4 %collective-permute-start.2 = (bf16[160,1408]{1,0:T(8,128)(2,1)S(1)}, bf16[160,1408]{1,0:T(8,128)(2,1)S(1)}, u32[]{:S(2)}, u32[]{:S(2)}) collective-permute-start(bf16[160,1408]{1,0:T(8,128)(2,1)S(1)} %pad_maximum_fusion.4), channel_id=1, source_target_pairs={{8,0},{10,2},{16,8},{18,10},{24,16},{26,18},{28,24},{30,26},{20,28... | collective-permute-start | bytes 1351688 | tf_op jit(solution)/shard_map/ppermute | solution.py:125
  46.4 21.3 %collective-permute-start.12 = (bf16[160,1408]{1,0:T(8,128)(2,1)S(1)}, bf16[160,1408]{1,0:T(8,128)(2,1)S(1)}, u32[]{:S(2)}, u32[]{:S(2)}) collective-permute-start(bf16[160,1408]{1,0:T(8,128)(2,1)S(1)} %collective-permute-done.1.refs_3_), channel_id=1, source_target_pairs={{0,8},{2,10},{8,16},{10,18},{16,24},{18,26},{24,28},{26,30},{28,20... | collective-permute-start | bytes 1351688 | tf_op jit(solution)/shard_map/ppermute | solution.py:125
  47.9 19.7 %collective-permute-start.13 = (bf16[160,1408]{1,0:T(8,128)(2,1)S(1)}, bf16[160,1408]{1,0:T(8,128)(2,1)S(1)}, u32[]{:S(2)}, u32[]{:S(2)}) collective-permute-start(bf16[160,1408]{1,0:T(8,128)(2,1)S(1)} %collective-permute-done.2.refs_4_), channel_id=1, source_target_pairs={{8,0},{10,2},{16,8},{18,10},{24,16},{26,18},{28,24},{30,26},{20,28... | collective-permute-start | bytes 1351688 | tf_op jit(solution)/shard_map/ppermute | solution.py:125
  58.0 29.0 %collective-permute-start.11 = (bf16[320,1408]{1,0:T(8,128)(2,1)}, bf16[320,1408]{1,0:T(8,128)(2,1)S(1)}, u32[]{:S(2)}, u32[]{:S(2)}) collective-permute-start(bf16[320,1408]{1,0:T(8,128)(2,1)} %pad_maximum_fusion.refs_3_), channel_id=1, source_target_pairs={{0,8},{2,10},{8,16},{10,18},{16,24},{18,26},{24,28},{26,30},{28,20... | collective-permute-start | bytes 2703368 | tf_op jit(solution)/shard_map/ppermute | solution.py:125
  69.3 41.7 %collective-permute-start.29 = (bf16[320,1408]{1,0:T(8,128)(2,1)S(1)}, bf16[320,1408]{1,0:T(8,128)(2,1)S(1)}, u32[]{:S(2)}, u32[]{:S(2)}) collective-permute-start(bf16[320,1408]{1,0:T(8,128)(2,1)S(1)} %pad_maximum_fusion.1.refs_2_), channel_id=1, source_target_pairs={{8,0},{10,2},{16,8},{18,10},{24,16},{26,18},{28,24},{30,26},{20,28... | collective-permute-start | bytes 2703368 | tf_op jit(solution)/shard_map/ppermute | solution.py:125
  69.8 26.8 %collective-permute-start.21 = (bf16[160,1408]{1,0:T(8,128)(2,1)S(1)}, bf16[160,1408]{1,0:T(8,128)(2,1)S(1)}, u32[]{:S(2)}, u32[]{:S(2)}) collective-permute-start(bf16[160,1408]{1,0:T(8,128)(2,1)S(1)} %collective-permute-done.12.refs_3_), channel_id=1, source_target_pairs={{0,8},{2,10},{8,16},{10,18},{16,24},{18,26},{24,28},{26,30},{28,20... | collective-permute-start | bytes 1351688 | tf_op jit(solution)/shard_map/ppermute | solution.py:125
  71.3 35.0 %collective-permute-start.20 = (bf16[160,1408]{1,0:T(8,128)(2,1)S(1)}, bf16[160,1408]{1,0:T(8,128)(2,1)S(1)}, u32[]{:S(2)}, u32[]{:S(2)}) collective-permute-start(bf16[160,1408]{1,0:T(8,128)(2,1)S(1)} %collective-permute-done.10.refs_2_), channel_id=1, source_target_pairs={{0,8},{2,10},{8,16},{10,18},{16,24},{18,26},{24,28},{26,30},{28,20... | collective-permute-start | bytes 1351688 | tf_op jit(solution)/shard_map/ppermute | solution.py:125
  72.6 33.7 %collective-permute-start.22 = (bf16[160,1408]{1,0:T(8,128)(2,1)S(1)}, bf16[160,1408]{1,0:T(8,128)(2,1)S(1)}, u32[]{:S(2)}, u32[]{:S(2)}) collective-permute-start(bf16[160,1408]{1,0:T(8,128)(2,1)S(1)} %collective-permute-done.13.refs_4_), channel_id=1, source_target_pairs={{8,0},{10,2},{16,8},{18,10},{24,16},{26,18},{28,24},{30,26},{20,28... | collective-permute-start | bytes 1351688 | tf_op jit(solution)/shard_map/ppermute | solution.py:125
  87.0 24.0 %collective-permute-start.23 = (bf16[160,1408]{1,0:T(8,128)(2,1)S(1)}, bf16[160,1408]{1,0:T(8,128)(2,1)S(1)}, u32[]{:S(2)}, u32[]{:S(2)}) collective-permute-start(bf16[160,1408]{1,0:T(8,128)(2,1)S(1)} %collective-permute-done.14.refs_5_), channel_id=1, source_target_pairs={{8,0},{10,2},{16,8},{18,10},{24,16},{26,18},{28,24},{30,26},{20,28... | collective-permute-start | bytes 1351688 | tf_op jit(solution)/shard_map/ppermute | solution.py:125
  96.6 28.0 %collective-permute-start.19 = (bf16[320,1408]{1,0:T(8,128)(2,1)S(1)}, bf16[320,1408]{1,0:T(8,128)(2,1)S(1)}, u32[]{:S(2)}, u32[]{:S(2)}) collective-permute-start(bf16[320,1408]{1,0:T(8,128)(2,1)S(1)} %collective-permute-done.11.refs_2_), channel_id=1, source_target_pairs={{0,8},{2,10},{8,16},{10,18},{16,24},{18,26},{24,28},{26,30},{28,20... | collective-permute-start | bytes 2703368 | tf_op jit(solution)/shard_map/ppermute | solution.py:125
  111.5 22.1 %collective-permute-start.30 = (bf16[320,1408]{1,0:T(8,128)(2,1)S(1)}, bf16[320,1408]{1,0:T(8,128)(2,1)S(1)}, u32[]{:S(2)}, u32[]{:S(2)}) collective-permute-start(bf16[320,1408]{1,0:T(8,128)(2,1)S(1)} %collective-permute-done.29.refs_3_), channel_id=1, source_target_pairs={{8,0},{10,2},{16,8},{18,10},{24,16},{26,18},{28,24},{30,26},{20,28... | collective-permute-start | bytes 2703368 | tf_op jit(solution)/shard_map/ppermute | solution.py:125
  124.7 21.1 %collective-permute-start.28 = (bf16[320,1408]{1,0:T(8,128)(2,1)S(1)}, bf16[320,1408]{1,0:T(8,128)(2,1)S(1)}, u32[]{:S(2)}, u32[]{:S(2)}) collective-permute-start(bf16[320,1408]{1,0:T(8,128)(2,1)S(1)} %collective-permute-done.19.refs_2_), channel_id=1, source_target_pairs={{0,8},{2,10},{8,16},{10,18},{16,24},{18,26},{24,28},{26,30},{28,20... | collective-permute-start | bytes 2703368 | tf_op jit(solution)/shard_map/ppermute | solution.py:125
  126.2 22.6 %collective-permute-start.37 = (bf16[320,1408]{1,0:T(8,128)(2,1)S(1)}, bf16[320,1408]{1,0:T(8,128)(2,1)S(1)}, u32[]{:S(2)}, u32[]{:S(2)}) collective-permute-start(bf16[320,1408]{1,0:T(8,128)(2,1)S(1)} %collective-permute-done.29.refs_3_), channel_id=1, source_target_pairs={{0,2},{2,0},{4,6},{6,4},{8,10},{10,8},{12,14},{14,12},{16,18},{18,... | collective-permute-start | bytes 2703368 | tf_op jit(solution)/shard_map/ppermute | solution.py:128
  126.2 23.1 %collective-permute-start.36 = (bf16[320,1408]{1,0:T(8,128)(2,1)S(1)}, bf16[320,1408]{1,0:T(8,128)(2,1)S(1)}, u32[]{:S(2)}, u32[]{:S(2)}) collective-permute-start(bf16[320,1408]{1,0:T(8,128)(2,1)S(1)} %collective-permute-done.11.refs_2_), channel_id=1, source_target_pairs={{0,2},{2,0},{4,6},{6,4},{8,10},{10,8},{12,14},{14,12},{16,18},{18,... | collective-permute-start | bytes 2703368 | tf_op jit(solution)/shard_map/ppermute | solution.py:128
  133.7 22.9 %collective-permute-start.31 = (bf16[320,1408]{1,0:T(8,128)(2,1)S(1)}, bf16[320,1408]{1,0:T(8,128)(2,1)S(1)}, u32[]{:S(2)}, u32[]{:S(2)}) collective-permute-start(bf16[320,1408]{1,0:T(8,128)(2,1)S(1)} %collective-permute-done.30.refs_3_), channel_id=1, source_target_pairs={{8,0},{10,2},{16,8},{18,10},{24,16},{26,18},{28,24},{30,26},{20,28... | collective-permute-start | bytes 2703368 | tf_op jit(solution)/shard_map/ppermute | solution.py:125
  147.3 18.6 %collective-permute-start.52 = (bf16[160,1408]{1,0:T(8,128)(2,1)S(1)}, bf16[160,1408]{1,0:T(8,128)(2,1)S(1)}, u32[]{:S(2)}, u32[]{:S(2)}) collective-permute-start(bf16[160,1408]{1,0:T(8,128)(2,1)S(1)} %collective-permute-done.21.refs_3_), channel_id=1, source_target_pairs={{0,8},{2,10},{8,16},{10,18},{16,24},{18,26},{24,28},{26,30},{28,20... | collective-permute-start | bytes 1351688 | tf_op jit(solution)/shard_map/ppermute | solution.py:125
  149.4 30.8 %collective-permute-start.35 = (bf16[320,1408]{1,0:T(8,128)(2,1)S(1)}, bf16[320,1408]{1,0:T(8,128)(2,1)S(1)}, u32[]{:S(2)}, u32[]{:S(2)}) collective-permute-start(bf16[320,1408]{1,0:T(8,128)(2,1)S(1)} %collective-permute-done.30.refs_3_), channel_id=1, source_target_pairs={{0,2},{2,0},{4,6},{6,4},{8,10},{10,8},{12,14},{14,12},{16,18},{18,... | collective-permute-start | bytes 2703368 | tf_op jit(solution)/shard_map/ppermute | solution.py:128
  156.6 24.1 %collective-permute-start.34 = (bf16[320,1408]{1,0:T(8,128)(2,1)S(1)}, bf16[320,1408]{1,0:T(8,128)(2,1)S(1)}, u32[]{:S(2)}, u32[]{:S(2)}) collective-permute-start(bf16[320,1408]{1,0:T(8,128)(2,1)S(1)} %collective-permute-done.19.refs_2_), channel_id=1, source_target_pairs={{0,2},{2,0},{4,6},{6,4},{8,10},{10,8},{12,14},{14,12},{16,18},{18,... | collective-permute-start | bytes 2703368 | tf_op jit(solution)/shard_map/ppermute | solution.py:128
  159.0 23.2 %collective-permute-start.32 = (bf16[320,1408]{1,0:T(8,128)(2,1)S(1)}, bf16[320,1408]{1,0:T(8,128)(2,1)S(1)}, u32[]{:S(2)}, u32[]{:S(2)}) collective-permute-start(bf16[320,1408]{1,0:T(8,128)(2,1)S(1)} %collective-permute-done.28.refs_2_), channel_id=1, source_target_pairs={{0,2},{2,0},{4,6},{6,4},{8,10},{10,8},{12,14},{14,12},{16,18},{18,... | collective-permute-start | bytes 2703368 | tf_op jit(solution)/shard_map/ppermute | solution.py:128
  165.9 22.2 %collective-permute-start.33 = (bf16[320,1408]{1,0:T(8,128)(2,1)S(1)}, bf16[320,1408]{1,0:T(8,128)(2,1)S(1)}, u32[]{:S(2)}, u32[]{:S(2)}) collective-permute-start(bf16[320,1408]{1,0:T(8,128)(2,1)S(1)} %collective-permute-done.31.refs_3_), channel_id=1, source_target_pairs={{0,2},{2,0},{4,6},{6,4},{8,10},{10,8},{12,14},{14,12},{16,18},{18,... | collective-permute-start | bytes 2703368 | tf_op jit(solution)/shard_map/ppermute | solution.py:128
  180.2 21.4 %collective-permute-start.43 = (bf16[160,1408]{1,0:T(8,128)(2,1)S(1)}, bf16[160,1408]{1,0:T(8,128)(2,1)S(1)}, u32[]{:S(2)}, u32[]{:S(2)}) collective-permute-start(bf16[160,1408]{1,0:T(8,128)(2,1)S(1)} %collective-permute-done.22.refs_4_), channel_id=1, source_target_pairs={{0,1},{1,0},{2,3},{3,2},{4,5},{5,4},{6,7},{7,6},{8,9},{9,8},{10,11... | collective-permute-start | bytes 1351688 | tf_op jit(solution)/shard_map/ppermute | solution.py:172
  180.7 30.5 %collective-permute-start.41 = (bf16[160,1408]{1,0:T(8,128)(2,1)S(1)}, bf16[160,1408]{1,0:T(8,128)(2,1)S(1)}, u32[]{:S(2)}, u32[]{:S(2)}) collective-permute-start(bf16[160,1408]{1,0:T(8,128)(2,1)S(1)} %collective-permute-done.21.refs_3_), channel_id=1, source_target_pairs={{0,1},{1,0},{2,3},{3,2},{4,5},{5,4},{6,7},{7,6},{8,9},{9,8},{10,11... | collective-permute-start | bytes 1351688 | tf_op jit(solution)/shard_map/ppermute | solution.py:172
  182.2 38.7 %collective-permute-start.39 = (bf16[160,1408]{1,0:T(8,128)(2,1)S(1)}, bf16[160,1408]{1,0:T(8,128)(2,1)S(1)}, u32[]{:S(2)}, u32[]{:S(2)}) collective-permute-start(bf16[160,1408]{1,0:T(8,128)(2,1)S(1)} %collective-permute-done.20.refs_2_), channel_id=1, source_target_pairs={{0,1},{1,0},{2,3},{3,2},{4,5},{5,4},{6,7},{7,6},{8,9},{9,8},{10,11... | collective-permute-start | bytes 1351688 | tf_op jit(solution)/shard_map/ppermute | solution.py:172
  194.0 64.2 %collective-permute-start.38 = (bf16[640,1408]{1,0:T(8,128)(2,1)S(1)}, bf16[640,1408]{1,0:T(8,128)(2,1)S(1)}, u32[]{:S(2)}, u32[]{:S(2)}) collective-permute-start(bf16[640,1408]{1,0:T(8,128)(2,1)S(1)} %shard_map.34), channel_id=1, source_target_pairs={{0,1},{1,0},{2,3},{3,2},{4,5},{5,4},{6,7},{7,6},{8,9},{9,8},{10,11... | collective-permute-start | bytes 5406728 | tf_op jit(solution)/shard_map/ppermute | solution.py:190
  195.6 25.3 %collective-permute-start.55 = (bf16[160,1408]{1,0:T(8,128)(2,1)S(1)}, bf16[160,1408]{1,0:T(8,128)(2,1)S(1)}, u32[]{:S(2)}, u32[]{:S(2)}) collective-permute-start(bf16[160,1408]{1,0:T(8,128)(2,1)S(1)} %collective-permute-done.51.refs_2_), channel_id=1, source_target_pairs={{0,2},{2,0},{4,6},{6,4},{8,10},{10,8},{12,14},{14,12},{16,18},{18,... | collective-permute-start | bytes 1351688 | tf_op jit(solution)/shard_map/ppermute | solution.py:128
  201.6 19.8 %collective-permute-start.56 = (bf16[160,1408]{1,0:T(8,128)(2,1)S(1)}, bf16[160,1408]{1,0:T(8,128)(2,1)S(1)}, u32[]{:S(2)}, u32[]{:S(2)}) collective-permute-start(bf16[160,1408]{1,0:T(8,128)(2,1)S(1)} %collective-permute-done.52.refs_3_), channel_id=1, source_target_pairs={{0,2},{2,0},{4,6},{6,4},{8,10},{10,8},{12,14},{14,12},{16,18},{18,... | collective-permute-start | bytes 1351688 | tf_op jit(solution)/shard_map/ppermute | solution.py:128
  221.4 21.9 %collective-permute-start.44 = (bf16[160,1408]{1,0:T(8,128)(2,1)S(1)}, bf16[160,1408]{1,0:T(8,128)(2,1)S(1)}, u32[]{:S(2)}, u32[]{:S(2)}) collective-permute-start(bf16[160,1408]{1,0:T(8,128)(2,1)S(1)} %collective-permute-done.43), channel_id=1, source_target_pairs={{8,0},{10,2},{16,8},{18,10},{24,16},{26,18},{28,24},{30,26},{20,28... | collective-permute-start | bytes 1351688 | tf_op jit(solution)/shard_map/ppermute | solution.py:125
  223.0 20.3 %collective-permute-start.42 = (bf16[160,1408]{1,0:T(8,128)(2,1)S(1)}, bf16[160,1408]{1,0:T(8,128)(2,1)S(1)}, u32[]{:S(2)}, u32[]{:S(2)}) collective-permute-start(bf16[160,1408]{1,0:T(8,128)(2,1)S(1)} %collective-permute-done.41), channel_id=1, source_target_pairs={{0,8},{2,10},{8,16},{10,18},{16,24},{18,26},{24,28},{26,30},{28,20... | collective-permute-start | bytes 1351688 | tf_op jit(solution)/shard_map/ppermute | solution.py:125
  223.5 21.4 %collective-permute-start.40 = (bf16[160,1408]{1,0:T(8,128)(2,1)S(1)}, bf16[160,1408]{1,0:T(8,128)(2,1)S(1)}, u32[]{:S(2)}, u32[]{:S(2)}) collective-permute-start(bf16[160,1408]{1,0:T(8,128)(2,1)S(1)} %collective-permute-done.39), channel_id=1, source_target_pairs={{0,8},{2,10},{8,16},{10,18},{16,24},{18,26},{24,28},{26,30},{28,20... | collective-permute-start | bytes 1351688 | tf_op jit(solution)/shard_map/ppermute | solution.py:125
  (31 other events, 309.1 us)
